TPU v7x, 512 devices: a whole 4x4x16 slice. The times are simulated.
512 devices in a mesh: gx: 16 (over z), gy: 32 (over x, y, core).
Axes of the slice: x: 4, y: 4, z: 16, core: 2. Of those that a mesh axis runs over, the one named last changes fastest.
Arguments:
- right_side: float32 [128, 512, 128], P('gx', 'gy'), may hold values from -8 to 8
- diagonal: float32 [128, 512, 128], P('gx', 'gy'), may hold values from 0.25 to 2
- solid_mask: int32 [128, 512, 128], P('gx', 'gy'), may hold values 0 or 1
- geneo_vectors: bfloat16 [32, 128, 512, 128], P(None, 'gx', 'gy'), may hold values from -0.046875 to 0.046875
- vector_counts: int32 [16, 32], P('gx', 'gy'), may hold values from 8 to 32, as said below
- owner_slots: int32 [512], replicated, may hold values from 0 to 511, each once
- coarse_inverse: float32 [16384, 1024], P('gy'), may hold values from -1 to 8, as said below
Outputs:
- solution: float32 [128, 512, 128], P('gx', 'gy')
- residual: float32 [128, 512, 128], P('gx', 'gy')
Inputs may be any that keep to these rules, and one draw needn't show every extreme that they name: `vector_counts`: every count lies between 8 and 32; both ends occur in every draw. Subdomain s belongs to coarse block owner_slots[s] // 32. `coarse_inverse`: each block is symmetric positive definite; rows and columns beyond a subdomain's count are unused.
All inputs are finite; a program needn't handle non-finite values. No bound on the sum of `solid_mask` on one device may be relied on, other than what follows from the above.
Results may differ from a plain program's by a relative error of at most 0.0003.
Values sent between devices are 32-bit elements; how exact they have to be, the bound alone decides.
A program may use at most 64 MiB of HBM per device.

v0:
```python
import jax
import jax.numpy as jnp
from jax import lax
from jax.sharding import PartitionSpec as P

DEG = 3
ITERS = 2


CHEB_LO = 0.3
CHEB_HI = 2.0
HIGH = lax.Precision.HIGHEST


def with_halo(cells, sides, width):
    for axis, dim in sides:
        count = lax.axis_size(axis)
        ends = count - 1
        head = lax.slice_in_dim(cells, 0, width, axis=dim)
        tail = lax.slice_in_dim(cells, cells.shape[dim] - width, cells.shape[dim], axis=dim)
        cells = jnp.concatenate(
            [
                lax.ppermute(tail, axis, [(i, (i + 1) % count) for i in range(ends)]),
                cells,
                lax.ppermute(head, axis, [((i + 1) % count, i) for i in range(ends)]),
            ],
            axis=dim,
        )
    return cells


def operate(field, diagonal, fluid):
    masked = fluid * field
    padded = with_halo(masked, (("gx", 0), ("gy", 1)), 1)
    beside = padded[2:, 1:-1] + padded[:-2, 1:-1] + padded[1:-1, 2:] + padded[1:-1, :-2]
    vertical = jnp.pad(masked, ((0, 0), (0, 0), (1, 1)))
    beside = beside + vertical[:, :, 2:] + vertical[:, :, :-2]
    return fluid * ((6.0 + diagonal) * field - beside) + (1.0 - fluid) * field


def smoother(res, diagonal, fluid, jacobi):
    centre = (CHEB_HI + CHEB_LO) / 2.0
    half_width = (CHEB_HI - CHEB_LO) / 2.0
    sigma_val = centre / half_width
    rho_old = 1.0 / sigma_val
    update = jacobi * res / centre
    smooth = update
    remainder = res
    for repeat in range(DEG - 1):
        remainder = remainder - operate(update, diagonal, fluid)
        rho_new = 1.0 / (2.0 * sigma_val - rho_old)
        update = rho_new * rho_old * update + 2.0 * rho_new / half_width * jacobi * remainder
        smooth = smooth + update
        rho_old = rho_new
    return smooth


def on_device(
    right_side, diagonal, solid_mask, geneo_vectors, vector_counts, owner_slots, coarse_inverse
):
    fluid = 1.0 - solid_mask.astype(jnp.float32)
    jacobi = 1.0 / (fluid * (6.0 + diagonal) + 1.0 - fluid)
    kcount = geneo_vectors.shape[0]
    shape_cells = right_side.shape
    live = (jnp.arange(kcount, dtype=jnp.int32) < vector_counts[0, 0]).astype(jnp.float32)
    vec_matrix = geneo_vectors.reshape(kcount, -1).astype(jnp.float32) * live[:, None]
    row_count = coarse_inverse.shape[0]
    block_len = coarse_inverse.shape[1]
    size_gy = lax.axis_size("gy")
    index_gx = lax.axis_index("gx")
    index_gy = lax.axis_index("gy")
    my_sub = index_gx * size_gy + index_gy
    my_slot = lax.dynamic_slice_in_dim(owner_slots, my_sub, 1, 0)[0]

    def precondition(res):
        smooth = smoother(res, diagonal, fluid, jacobi)
        projected = jnp.dot(vec_matrix, res.reshape(-1), precision=HIGH)
        every_rhs = lax.all_gather(projected[None, :], ("gx", "gy"), axis=0, tiled=True)
        ordered = jnp.zeros(every_rhs.shape, jnp.float32).at[owner_slots].set(every_rhs)
        ordered_blocks = ordered.reshape(-1, block_len)
        first_row = index_gy * row_count
        row_ids = first_row + jnp.arange(row_count, dtype=jnp.int32)
        picked = ordered_blocks[row_ids // block_len]
        coarse_part = jnp.sum(coarse_inverse * picked, axis=1)
        coarse_full = lax.all_gather(coarse_part, "gy", axis=0, tiled=True)
        coeffs = lax.dynamic_slice_in_dim(coarse_full.reshape(-1, kcount), my_slot, 1, 0)[0] * live
        fine = jnp.dot(coeffs, vec_matrix, precision=HIGH)
        inner = None
        return (smooth + fine.reshape(shape_cells), inner)

    def residual_product(resid, pre):
        return lax.psum(jnp.sum(resid * pre), ("gx", "gy"))

    solution = jnp.zeros_like(right_side)
    residual = right_side
    precond, inner = precondition(residual)
    direction = precond
    norm_now = residual_product(residual, precond)
    for repeat in range(ITERS):
        image = operate(direction, diagonal, fluid)
        curvature = lax.psum(jnp.sum(direction * image), ("gx", "gy"))
        step_len = norm_now / curvature
        solution = solution + step_len * direction
        residual = residual - step_len * image
        if repeat + 1 < ITERS:
            precond, inner = precondition(residual)
            norm_next = residual_product(residual, precond)
            direction = precond + norm_next / norm_now * direction
            norm_now = norm_next
    return (solution, residual)


def solution(mesh):
    in_specs = (
        P("gx", "gy", None),
        P("gx", "gy", None),
        P("gx", "gy", None),
        P(None, "gx", "gy", None),
        P("gx", "gy"),
        P(),
        P("gy", None),
    )
    out_specs = (P("gx", "gy", None), P("gx", "gy", None))
    return jax.shard_map(
        on_device, mesh=mesh, in_specs=in_specs, out_specs=out_specs, check_vma=False
    )
```

profile of v0, /device:TPU:1, one launch (start us, length us, event | category | flops | bytes accessed | tf_op | source)
XLA Modules:
  0.0 1346.5 jit_solution(2182651095264097952)
XLA Ops:
  7.9 1.5 broadcast_multiply_fusion
  9.5 2.8 fusion.9
  13.3 1.3 collective-permute-start
  14.6 5.0 collective-permute-start.1
  19.9 2.5 fusion
  22.4 4.1 collective-permute-start.3
  26.6 5.5 collective-permute-start.2
  33.0 1.3 collective-permute-start.4
  34.3 4.0 collective-permute-start.5
  40.2 3.3 copy.20
  44.2 1.9 collective-permute-start.7
  46.1 2.4 collective-permute-start.6
  48.5 411.5 %all-reduce.12.cloned.1.call-done = f32[16384]{0:T(1024)} async-done(((f32[16384]{0:T(1024)}), f32[16384]{0:T(1024)}) %all-reduce.12.cloned.1.call-update) | async-done | bytes 65552
  460.0 0.9 reshape.138
  461.0 1.8 scatter_custom_fusion
  462.9 2.7 gather_fusion
  465.6 2.5 multiply_reduce_fusion.1
  468.1 24.3 %all-gather.2 = f32[32,1,512]{2,1,0:T(1,128)S(1)} all-gather(f32[1,1,512]{2,1,0:T(1,128)S(1)} %bitcast.63), channel_id=1, replica_groups=mesh['gx'=16,'gy'=32] {'gy'}, dimensions={0}, use_global_device_ids=true | all-gather | bytes 67584 | tf_op jit(solution)/shard_map/all_gather | solution.py:85
  492.7 3.8 fusion.3
  496.7 1.3 collective-permute-start.8
  498.0 4.0 collective-permute-start.9
  502.8 3.8 collective-permute-start.11
  506.6 1.9 collective-permute-start.10
  508.6 3.0 collective-permute-done.10
  512.3 103.6 %all-reduce.8 = (f32[]{:T(128)}, f32[]{:T(128)}) all-reduce(f32[]{:T(128)} %get-tuple-element.3, f32[]{:T(128)} %get-tuple-element.2), channel_id=1, replica_groups=mesh['gx'=16,'gy'=32] {'gx','gy'}, use_global_device_ids=true, to_apply=%region_3.4 | all-reduce | flops 2 | bytes 16 | tf_op jit(solution)/shard_map/psum | solution.py:92
  617.2 1.3 collective-permute-start.12
  618.5 4.0 collective-permute-start.13
  623.2 3.8 collective-permute-start.15
  627.0 1.9 collective-permute-start.14
  629.0 3.0 collective-permute-done.14
  632.1 1.3 collective-permute-start.16
  633.4 4.5 collective-permute-start.17
  638.0 2.8 fusion.12
  641.7 2.2 collective-permute-start.19
  643.9 2.1 collective-permute-start.18
  646.0 436.5 %all-reduce.14.cloned.1.call-done = f32[16384]{0:T(1024)} async-done(((f32[16384]{0:T(1024)}), f32[16384]{0:T(1024)}) %all-reduce.14.cloned.1.call-update) | async-done | bytes 65552
  1083.5 1.8 scatter_custom_fusion.1
  1085.4 2.7 gather_fusion.1
  1088.1 2.6 multiply_reduce_fusion
  1090.8 24.3 %all-gather.3 = f32[32,1,512]{2,1,0:T(1,128)S(1)} all-gather(f32[1,1,512]{2,1,0:T(1,128)S(1)} %bitcast.64), channel_id=1, replica_groups=mesh['gx'=16,'gy'=32] {'gy'}, dimensions={0}, use_global_device_ids=true | all-gather | bytes 67584 | tf_op jit(solution)/shard_map/all_gather | solution.py:85
  1115.4 2.2 fusion.1
  1118.4 99.4 %psum.30 = f32[]{:T(128)} all-reduce(f32[]{:T(128)} %get-tuple-element.10), channel_id=1, replica_groups=mesh['gx'=16,'gy'=32] {'gx','gy'}, use_global_device_ids=true, to_apply=%region_9.10 | all-reduce | flops 1 | bytes 8 | tf_op jit(solution)/shard_map/psum | solution.py:92
  1219.1 1.3 collective-permute-start.20
  1220.4 4.3 collective-permute-start.21
  1225.5 3.9 collective-permute-start.23
  1229.5 1.9 collective-permute-start.22
  1231.4 3.0 collective-permute-done.22
  1235.1 102.5 %psum.31 = f32[]{:T(128)} all-reduce(f32[]{:T(128)} %get-tuple-element.6), channel_id=1, replica_groups=mesh['gx'=16,'gy'=32] {'gx','gy'}, use_global_device_ids=true, to_apply=%region_11.12 | all-reduce | flops 1 | bytes 8 | tf_op jit(solution)/shard_map/psum | solution.py:101
  (80 shorter events, 11.2 us)
Async XLA Ops:
  7.2 2.3 copy-start.4
  7.2 452.9 %all-reduce.12.cloned.1.call-start = ((), (), s32[]{:S(2)}) async-start(), calls=%async_computation | async-start | bytes 131072
  7.9 5.3 copy-start.1
  7.9 5.3 copy-start.3
  7.9 11.7 copy-start.2
  12.5 0.6 copy-start.6
  13.2 1069.4 %all-reduce.14.cloned.1.call-start = ((), (), s32[]{:S(2)}) async-start(), calls=%async_computation.1 | async-start | bytes 131072
  13.3 9.1 collective-permute-start
  14.6 7.8 collective-permute-start.1
  19.8 2.5 copy-start.7
  22.4 9.7 collective-permute-start.3
  26.6 6.3 collective-permute-start.2
  33.0 11.1 collective-permute-start.4
  34.3 9.9 collective-permute-start.5
  44.2 452.3 %collective-permute-start.7 = (f32[10,1,128]{2,1,0:T(1,128)S(1)}, f32[10,1,128]{2,1,0:T(1,128)S(1)}, u32[]{:S(2)}, u32[]{:S(2)}) collective-permute-start(f32[10,1,128]{2,1,0:T(1,128)S(1)} %get-tuple-element.26), channel_id=1, source_target_pairs={{0,1},{1,2},{2,3},{3,4},{4,5},{5,6},{6,7},{7,8},{8,9},{9,10},{10,1... | collective-permute-start | bytes 15368 | tf_op jit(solution)/shard_map/ppermute | solution.py:23
  46.1 450.4 %collective-permute-start.6 = (f32[10,1,128]{2,1,0:T(1,128)S(1)}, f32[10,1,128]{2,1,0:T(1,128)S(1)}, u32[]{:S(2)}, u32[]{:S(2)}) collective-permute-start(f32[10,1,128]{2,1,0:T(1,128)S(1)} %get-tuple-element.25), channel_id=1, source_target_pairs={{1,0},{2,1},{3,2},{4,3},{5,4},{6,5},{7,6},{8,7},{9,8},{10,9},{11,1... | collective-permute-start | bytes 15368 | tf_op jit(solution)/shard_map/ppermute | solution.py:25
  496.7 5.3 collective-permute-start.8
  498.0 4.8 collective-permute-start.9
  502.8 5.8 collective-permute-start.11
  506.6 4.9 collective-permute-start.10
  617.2 5.3 collective-permute-start.12
  618.5 4.8 collective-permute-start.13
  623.2 5.7 collective-permute-start.15
  627.0 4.9 collective-permute-start.14
  632.1 9.6 collective-permute-start.16
  633.4 8.3 collective-permute-start.17
  641.0 0.6 copy-start.5
  641.7 475.9 %collective-permute-start.19 = (f32[10,1,128]{2,1,0:T(1,128)S(1)}, f32[10,1,128]{2,1,0:T(1,128)S(1)}, u32[]{:S(2)}, u32[]{:S(2)}) collective-permute-start(f32[10,1,128]{2,1,0:T(1,128)S(1)} %get-tuple-element.20), channel_id=1, source_target_pairs={{0,1},{1,2},{2,3},{3,4},{4,5},{5,6},{6,7},{7,8},{8,9},{9,10},{10,1... | collective-permute-start | bytes 15368 | tf_op jit(solution)/shard_map/ppermute | solution.py:23
  643.9 473.7 %collective-permute-start.18 = (f32[10,1,128]{2,1,0:T(1,128)S(1)}, f32[10,1,128]{2,1,0:T(1,128)S(1)}, u32[]{:S(2)}, u32[]{:S(2)}) collective-permute-start(f32[10,1,128]{2,1,0:T(1,128)S(1)} %get-tuple-element.19), channel_id=1, source_target_pairs={{1,0},{2,1},{3,2},{4,3},{5,4},{6,5},{7,6},{8,7},{9,8},{10,9},{11,1... | collective-permute-start | bytes 15368 | tf_op jit(solution)/shard_map/ppermute | solution.py:25
  1088.1 27.3 %copy-start = (f32[4,8,128,128]{3,2,1,0:T(8,128)S(1)}, f32[4,8,128,128]{3,2,1,0:T(8,128)}, u32[]{:S(2)}) copy-start(f32[4,8,128,128]{3,2,1,0:T(8,128)} %copy.20) | copy-start | bytes 6291460
  1219.1 5.6 collective-permute-start.20
  1220.4 5.1 collective-permute-start.21
  1225.5 5.9 collective-permute-start.23
  1229.5 4.9 collective-permute-start.22
Sparse Core Ops, SparseCore 0:
  14.0 445.9 all-reduce.11
  641.8 440.7 all-reduce.13
where the time goes:
time: 1350 us
  waiting for transfers between devices  860 us (64%)
  blocking collectives  354 us (26%)
  starting transfers between devices  69.2 us (5%)
  between operations  21.1 us (2%)
  local copies, waits for them, and re-layouts  17.1 us (1%)
    unnamed x4, waiting for transfers between devices  848 us
    psum x2, blocking collectives, residual_product(): return lax.psum(jnp.sum(resid * pre), ('gx', 'gy'))  203 us
    psum x1, blocking collectives, on_device(): curvature = lax.psum(jnp.sum(direction * image), ('gx', 'gy'))  103 us
    all_gather x2, blocking collectives, precondition(): coarse_full = lax.all_gather(coarse_part, 'gy', axis=0, tiled=True)  48.7 us
    ppermute x12, starting transfers between devices, with_halo(): lax.ppermute(tail, axis, [(i, (i + 1) % count) for i in range(ends)])  45.7 us
  transfers between devices with their start and end apart: 26, of which 9 were waited for; matrix products, arithmetic and copies ran while one was open for 2% of the time, Pallas kernels for 0%

commit v1 on v0

v1 whole, which is shorter than its diff:
```python
import functools

import jax
import jax.numpy as jnp
from jax import lax
from jax.experimental import pallas as pl
from jax.experimental.pallas import tpu as pltpu
from jax.sharding import PartitionSpec as P

CHEB_LO = 0.3
CHEB_HI = 2.0
THETA = (CHEB_HI + CHEB_LO) / 2.0
DELTA = (CHEB_HI - CHEB_LO) / 2.0
SIGMA = THETA / DELTA
HIGH = lax.Precision.HIGHEST
MESH = pl.DeviceIdType.MESH
F32 = jnp.float32


def lane_ids(shape):
    return lax.broadcasted_iota(jnp.int32, shape, len(shape) - 1)


def row_sums(rows):
    return lax.dot_general(
        jnp.ones((8, 128), F32), rows, (((1,), (1,)), ((), ())),
        precision=HIGH, preferred_element_type=F32,
    )


def kernel(
    nx, ny, kmax,
    right_hbm, diag_hbm, mask_hbm, vec_hbm, count_ref, slot_ref, slots_ref, inv_hbm,
    sol_ref, res_ref,
    right, diag, solid, vec, inv, fluid, jac, pad,
    parts, stack, onehot,
    zsend, zbuf, psend, pbuf, csend, cbuf,
    xsend, xbuf, ysend, ybuf,
    fsend, fzbuf, fpsend, fpbuf,
    load_sem, z_send_sem, z_recv_sem, p_send_sem, p_recv_sem, c_send_sem, c_recv_sem,
    h_send_sem, h_recv_sem, f_send_sem, f_recv_sem,
):
    gx, gy = lax.axis_index("gx"), lax.axis_index("gy")

    def along_x(step):
        return {"gx": lax.rem(gx + step, nx)}

    def along_y(step):
        return {"gy": lax.rem(gy + step, ny)}

    barrier = pltpu.get_barrier_semaphore()
    for step in range(1, nx):
        pl.semaphore_signal(barrier, inc=1, device_id=along_x(step), device_id_type=MESH)
    for step in range(1, ny):
        pl.semaphore_signal(barrier, inc=1, device_id=along_y(step), device_id_type=MESH)

    loads = [
        pltpu.make_async_copy(src, dst, load_sem.at[i])
        for i, (src, dst) in enumerate(
            [(right_hbm, right), (vec_hbm, vec), (mask_hbm, solid), (diag_hbm, diag), (inv_hbm, inv)]
        )
    ]
    for load in loads:
        load.start()

    count = count_ref[0, 0]
    lane = lane_ids((1, 128))
    live = ((lane < count) | (lane >= kmax)).astype(F32)

    def remote(src, dst, send_sem, recv_sem, device):
        return pltpu.make_async_remote_copy(
            src_ref=src, dst_ref=dst, send_sem=send_sem, recv_sem=recv_sem,
            device_id=device, device_id_type=MESH,
        )

    def wait_bytes(ref, sem):
        pltpu.make_async_copy(ref, ref, sem).wait()

    def fold(cells):
        total = jnp.sum(cells, axis=0)
        return total[0:8] + total[8:16]

    def z_start(n):
        for step in range(1, nx):
            remote(zsend.at[n], zbuf.at[n, gx], z_send_sem.at[n], z_recv_sem.at[n], along_x(step)).start()
        pltpu.make_async_copy(zsend.at[n], zbuf.at[n, gx], z_recv_sem.at[n]).start()

    def p_start(n):
        for step in range(1, ny):
            remote(psend.at[n], pbuf.at[n, :, pl.ds(gy, 1)], p_send_sem.at[n], p_recv_sem.at[n], along_y(step)).start()
        pltpu.make_async_copy(psend.at[n], pbuf.at[n, :, pl.ds(gy, 1)], p_recv_sem.at[n]).start()

    def c_start(n):
        for step in range(1, ny):
            remote(csend.at[n], cbuf.at[n, gy], c_send_sem.at[n], c_recv_sem.at[n], along_y(step)).start()
        pltpu.make_async_copy(csend.at[n], cbuf.at[n, gy], c_recv_sem.at[n]).start()

    def halo_copies(n):
        return [
            remote(xsend.at[n, 0], xbuf.at[n, 1], h_send_sem.at[n, 0], h_recv_sem.at[n, 0], along_x(nx - 1)),
            remote(xsend.at[n, 1], xbuf.at[n, 0], h_send_sem.at[n, 1], h_recv_sem.at[n, 1], along_x(1)),
            remote(ysend.at[n, 0], ybuf.at[n, 1], h_send_sem.at[n, 2], h_recv_sem.at[n, 2], along_y(ny - 1)),
            remote(ysend.at[n, 1], ybuf.at[n, 0], h_send_sem.at[n, 3], h_recv_sem.at[n, 3], along_y(1)),
        ]

    def halo_start(n, field):
        masked = fluid[...] * field
        pad[1:9, 8:24, :] = masked
        xsend[n, 0] = masked[0]
        xsend[n, 1] = masked[7]
        ysend[n, 0] = masked[:, 0, :]
        ysend[n, 1] = masked[:, 15, :]
        for copy in halo_copies(n):
            copy.start()

    def halo_finish(n, field):
        for copy in halo_copies(n):
            copy.wait_recv()
        zero = jnp.float32(0.0)
        keep = [gx > 0, gx < nx - 1, gy > 0, gy < ny - 1]
        scale = [jnp.where(k, jnp.float32(1.0), zero) for k in keep]
        pad[0, 8:24, :] = xbuf[n, 0] * scale[0]
        pad[9, 8:24, :] = xbuf[n, 1] * scale[1]
        pad[1:9, 7:8, :] = (ybuf[n, 0] * scale[2]).reshape(8, 1, 128)
        pad[1:9, 24:25, :] = (ybuf[n, 1] * scale[3]).reshape(8, 1, 128)
        masked = pad[1:9, 8:24, :]
        beside = pad[2:10, 8:24, :] + pad[0:8, 8:24, :]
        beside = beside + pad[1:9, 9:25, :] + pad[1:9, 7:23, :]
        lanes = lane_ids((8, 16, 128))
        beside = beside + jnp.where(lanes == 127, zero, pltpu.roll(masked, 127, 2))
        beside = beside + jnp.where(lanes == 0, zero, pltpu.roll(masked, 1, 2))
        fl = fluid[...]
        return fl * ((6.0 + diag[...]) * field - beside) + (1.0 - fl) * field

    def project(n, cells_ref, extras):
        def group(g, carry):
            cells = cells_ref[...]
            for j in range(4):
                k = g * 4 + j
                parts[k] = fold(vec[k].astype(F32) * cells)
            return carry

        lax.fori_loop(0, kmax // 4, group, 0)
        for i in range(8):
            parts[kmax + i] = extras[i] if i < len(extras) else jnp.zeros((8, 128), F32)
        stack[0:kmax + 8, :] = jnp.sum(parts[...], axis=1)
        zsend[n] = row_sums(stack[...])[0:1] * live

    def compact(n):
        rows = zbuf[n].reshape(nx, 128)
        low = jnp.where(lane_ids((nx, 128)) < kmax, rows, 0.0)
        packed = low[0:4]
        for a in range(1, 4):
            packed = packed + pltpu.roll(low[4 * a:4 * a + 4], 32 * a, 1)
        psend[n, 0:4] = packed.reshape(4, 1, 128)
        psend[n, 4] = jnp.sum(rows, axis=0, keepdims=True)

    def coarse(n):
        gathered = pbuf[n, 0:4].reshape(4 * ny, 128)
        picked = jnp.dot(onehot[...], gathered, precision=HIGH, preferred_element_type=F32)
        group = lane_ids((32, 128)) // 32
        own = jnp.zeros((32, 128), F32)
        for a in range(4):
            own = own + jnp.where(group == a, picked[32 * a:32 * a + 32], 0.0)
        own = own + pltpu.roll(own, 32, 1)
        own = own + pltpu.roll(own, 64, 1)
        group = lane_ids((8, 128)) // 32
        ordered = jnp.zeros((8, 128), F32)
        for q in range(4):
            ordered = ordered + jnp.where(group == q, own[8 * q:8 * q + 8], 0.0)
        for c in range(4):
            acc = inv[128 * c:128 * c + 128, 0:128] * ordered[0:1]
            for i in range(1, 8):
                acc = acc + inv[128 * c:128 * c + 128, 128 * i:128 * i + 128] * ordered[i:i + 1]
            csend[n, c:c + 1] = row_sums(acc)[0:1]

    def prolong(n):
        slot = slot_ref[gx * ny + gy]
        row = cbuf[n, slot // 16, pl.ds((slot // 4) % 4, 1), :]
        row = jnp.where(lane // 32 == slot % 4, row, 0.0)
        row = row + pltpu.roll(row, 32, 1)
        row = row + pltpu.roll(row, 64, 1)
        row = row * live
        total = jnp.zeros((8, 16, 128), F32)
        for k in range(kmax):
            weight = jnp.broadcast_to(row[:, k:k + 1], (1, 128)).reshape(1, 1, 128)
            total = total + vec[k].astype(F32) * weight
        return total

    rho = [1.0 / SIGMA]
    for _ in range(2):
        rho.append(1.0 / (2.0 * SIGMA - rho[-1]))

    def smooth_update(n, update, rest):
        return rho[n] * rho[n - 1] * update + (2.0 * rho[n] / DELTA) * jac[...] * rest

    def scalar(row, i):
        return jnp.broadcast_to(row[:, i:i + 1], (1, 128)).reshape(1, 1, 128)

    loads[0].wait()
    loads[1].wait()
    stack[...] = jnp.zeros((128, 128), F32)
    project(0, right, [])
    loads[2].wait()
    loads[3].wait()
    fl = 1.0 - solid[...].astype(F32)
    fluid[...] = fl
    jac[...] = 1.0 / (fl * (6.0 + diag[...]) + 1.0 - fl)
    pad[...] = jnp.zeros(pad.shape, F32)

    pl.semaphore_wait(barrier, nx - 1 + ny - 1)
    z_start(0)

    def apply_preconditioner(n, res, h, between=None):
        update = jac[...] * res / THETA
        halo_start(h, update)
        if n == 0:
            block = gy // 2
            want = lax.broadcasted_iota(jnp.int32, (32, 128), 0)
            want = 32 * block + 4 * (want % 8) + want // 8
            for a in range(4):
                have = slots_ref[pl.ds(128 * a, 128)].reshape(1, 128)
                onehot[32 * a:32 * a + 32, :] = (want == have).astype(F32)
        rest = res - halo_finish(h, update)
        smooth = update
        update = smooth_update(1, update, rest)
        smooth = smooth + update
        halo_start(h + 1, update)
        wait_bytes(zbuf.at[n], z_recv_sem.at[n])
        compact(n)
        p_start(n)
        rest = rest - halo_finish(h + 1, update)
        smooth = smooth + smooth_update(2, update, rest)
        if n == 0:
            loads[4].wait()
        wait_bytes(pbuf.at[n], p_recv_sem.at[n])
        coarse(n)
        c_start(n)
        sums = jnp.sum(pbuf[n, 4], axis=0, keepdims=True)
        wait_bytes(cbuf.at[n], c_recv_sem.at[n])
        return smooth + prolong(n), sums

    r0 = right[...]
    z0, _ = apply_preconditioner(0, r0, 0)
    sol_ref[...] = z0
    halo_start(2, z0)
    norm_part = fold(r0 * z0)
    q0 = halo_finish(2, z0)
    res_ref[...] = q0
    project(1, res_ref, [norm_part, fold(z0 * q0)])
    z_start(1)
    w0, sums = apply_preconditioner(1, q0, 3)
    norm0, curv0 = scalar(sums, kmax), scalar(sums, kmax + 1)
    step0 = norm0 / curv0
    z0, q0 = sol_ref[...], res_ref[...]
    z1 = z0 - step0 * w0
    r1 = right[...] - step0 * q0
    right[...] = r1
    halo_start(5, z1)
    parts[0] = fold(r1 * z1)
    parts[1] = fold(z1 * q0)
    t1 = halo_finish(5, z1)
    parts[2] = fold(z1 * t1)

    stack[0:8, :] = jnp.sum(parts[0:8], axis=1)
    fsend[...] = row_sums(stack[...])[0:1]
    for step in range(1, nx):
        remote(fsend, fzbuf.at[gx], f_send_sem.at[0], f_recv_sem.at[0], along_x(step)).start()
    pltpu.make_async_copy(fsend, fzbuf.at[gx], f_recv_sem.at[0]).start()
    wait_bytes(fzbuf, f_recv_sem.at[0])
    fpsend[...] = jnp.sum(fzbuf[...], axis=0)
    for step in range(1, ny):
        remote(fpsend, fpbuf.at[gy], f_send_sem.at[1], f_recv_sem.at[1], along_y(step)).start()
    pltpu.make_async_copy(fpsend, fpbuf.at[gy], f_recv_sem.at[1]).start()
    wait_bytes(fpbuf, f_recv_sem.at[1])
    last = jnp.sum(fpbuf[...], axis=0)
    norm1, cross, inner = scalar(last, 0), scalar(last, 1), scalar(last, 2)
    beta = norm1 / norm0
    step1 = norm1 / (inner + 2.0 * beta * cross + beta * beta * curv0)
    sol_ref[...] = (step0 + step1 * beta) * z0 + step1 * z1
    res_ref[...] = right[...] - step1 * (t1 + beta * q0)

    for n in range(2):
        wait_bytes(zbuf.at[n, pl.ds(0, nx - 1)], z_send_sem.at[n])
        wait_bytes(pbuf.at[n, :, pl.ds(0, ny - 1)], p_send_sem.at[n])
        wait_bytes(cbuf.at[n, pl.ds(0, ny - 1)], c_send_sem.at[n])
    for n in range(6):
        for copy in halo_copies(n):
            copy.wait_send()
    wait_bytes(fzbuf.at[pl.ds(0, nx - 1)], f_send_sem.at[0])
    wait_bytes(fpbuf.at[pl.ds(0, ny - 1)], f_send_sem.at[1])


def solution(mesh):
    nx, ny = mesh.shape["gx"], mesh.shape["gy"]

    def on_device(right_side, diagonal, solid_mask, vectors, counts, slots, inverse):
        cells = right_side.shape
        kmax = vectors.shape[0]
        hbm = pl.BlockSpec(memory_space=pl.ANY)
        smem = pl.BlockSpec(memory_space=pltpu.SMEM)
        vmem = pl.BlockSpec(memory_space=pltpu.VMEM)
        dma = pltpu.SemaphoreType.DMA
        out = jax.ShapeDtypeStruct(cells, F32)
        return pl.pallas_call(
            functools.partial(kernel, nx, ny, kmax),
            out_shape=(out, out),
            in_specs=[hbm, hbm, hbm, hbm, smem, smem, vmem, hbm],
            out_specs=(vmem, vmem),
            scratch_shapes=[
                pltpu.VMEM(cells, F32), pltpu.VMEM(cells, F32), pltpu.VMEM(cells, jnp.int32),
                pltpu.VMEM(vectors.shape, vectors.dtype), pltpu.VMEM(inverse.shape, F32),
                pltpu.VMEM(cells, F32), pltpu.VMEM(cells, F32), pltpu.VMEM((10, 32, 128), F32),
                pltpu.VMEM((kmax + 8, 8, 128), F32), pltpu.VMEM((128, 128), F32), pltpu.VMEM((128, 128), F32),
                pltpu.VMEM((2, 1, 128), F32), pltpu.VMEM((2, nx, 1, 128), F32),
                pltpu.VMEM((2, 5, 1, 128), F32), pltpu.VMEM((2, 5, ny, 128), F32),
                pltpu.VMEM((2, 4, 128), F32), pltpu.VMEM((2, ny, 4, 128), F32),
                pltpu.VMEM((6, 2, 16, 128), F32), pltpu.VMEM((6, 2, 16, 128), F32),
                pltpu.VMEM((6, 2, 8, 128), F32), pltpu.VMEM((6, 2, 8, 128), F32),
                pltpu.VMEM((1, 128), F32), pltpu.VMEM((nx, 1, 128), F32),
                pltpu.VMEM((1, 128), F32), pltpu.VMEM((ny, 1, 128), F32),
                dma((5,)), dma((2,)), dma((2,)), dma((2,)), dma((2,)), dma((2,)), dma((2,)),
                dma((6, 4)), dma((6, 4)), dma((2,)), dma((2,)),
            ],
            compiler_params=pltpu.CompilerParams(
                collective_id=0, has_side_effects=True, vmem_limit_bytes=32 * 1024 * 1024
            ),
            cost_estimate=pl.CostEstimate(flops=10_000_000, bytes_accessed=4_000_000, transcendentals=0),
        )(right_side, diagonal, solid_mask, vectors, counts, slots, slots, inverse)

    in_specs = (
        P("gx", "gy", None),
        P("gx", "gy", None),
        P("gx", "gy", None),
        P(None, "gx", "gy", None),
        P("gx", "gy"),
        P(),
        P("gy", None),
    )
    out_specs = (P("gx", "gy", None), P("gx", "gy", None))
    return jax.shard_map(
        on_device, mesh=mesh, in_specs=in_specs, out_specs=out_specs, check_vma=False
    )
```

time: 1350 us -> 82.2 us (0.06)
  waiting for transfers between devices: 860 us -> 0 us
  blocking collectives: 354 us -> 0 us
  Pallas kernels: 0 us -> 73.3 us
  starting transfers between devices: 69.2 us -> 0 us
  between operations: 21.1 us -> 1.3 us
    unnamed x4 -> x0, waiting for transfers between devices: 848 us -> none
    psum x3 -> x0, blocking collectives: 306 us -> none  [the longest x2 203 us: residual_product(): return lax.psum(jnp.sum(resid * pre), ('gx', 'gy'))]
    pallas_call x0 -> x1, Pallas kernels: none -> 73.3 us  [on_device(): pl.pallas_call(functools.partial(kernel, nx, ny, kmax), out_shape=(out, o...]
    ppermute x24 -> x0, starting transfers between devices: 69.2 us -> none  [the longest x12 45.7 us: with_halo(): lax.ppermute(tail, axis, [(i, (i + 1) % count) for i in range(ends)])]
    all_gather x2 -> x0, blocking collectives: 48.7 us -> none  [precondition(): coarse_full = lax.all_gather(coarse_part, 'gy', axis=0, tiled=True)]
  transfers between devices with their start and end apart: 26 -> 0, of which waited for: 9 -> 0; matrix products, arithmetic and copies ran while one was open for 2% -> 0% of each run, Pallas kernels for 0% -> 0%
where the time goes in v1:
time: 82.2 us; the launch traced here: 81.9 us
  Pallas kernels  73.3 us (89%)
  local copies, waits for them, and re-layouts  7.27 us (9%)
  between operations  1.3 us (2%)
    pallas_call x1, Pallas kernels, on_device(): pl.pallas_call(functools.partial(kernel, nx, ny, kmax), out_shape=(out, o...  73.3 us
    unnamed x14, local copies, waits for them, and re-layouts  7.27 us

profile of v1, /device:TPU:1, one launch (start us, length us, event | category | flops | bytes accessed | tf_op | source)
XLA Modules:
  0.0 81.9 jit_solution(2582668683530346385)
XLA Ops:
  1.3 0.0 copy-start
  1.3 1.6 %copy-done = f32[512,1024]{1,0:T(8,128)S(1)} copy-done((f32[512,1024]{1,0:T(8,128)S(1)}, f32[512,1024]{1,0:T(8,128)}, u32[]{:S(2)}) %copy-start) | copy-done | bytes 2097176
  2.9 0.0 copy-start.1
  2.9 1.2 %copy-done.1 = bf16[32,8,16,128]{3,2,1,0:T(8,128)(2,1)S(1)} copy-done((bf16[32,8,16,128]{3,2,1,0:T(8,128)(2,1)S(1)}, bf16[32,8,16,128]{3,2,1,0:T(8,128)(2,1)}, u32[]{:S(2)}) %copy-start.1) | copy-done | bytes 1048600
  4.1 0.0 copy-start.2
  4.1 0.8 %copy-done.2 = f32[8,16,128]{2,1,0:T(8,128)S(1)} copy-done((f32[8,16,128]{2,1,0:T(8,128)S(1)}, f32[8,16,128]{2,1,0:T(8,128)}, u32[]{:S(2)}) %copy-start.2) | copy-done | bytes 65560
  4.9 0.0 copy-start.3
  4.9 0.8 %copy-done.3 = f32[8,16,128]{2,1,0:T(8,128)S(1)} copy-done((f32[8,16,128]{2,1,0:T(8,128)S(1)}, f32[8,16,128]{2,1,0:T(8,128)}, u32[]{:S(2)}) %copy-start.3) | copy-done | bytes 65560
  5.8 0.0 copy-start.4
  5.8 0.8 %copy-done.4 = s32[8,16,128]{2,1,0:T(8,128)S(1)} copy-done((s32[8,16,128]{2,1,0:T(8,128)S(1)}, s32[8,16,128]{2,1,0:T(8,128)}, u32[]{:S(2)}) %copy-start.4) | copy-done | bytes 65560
  6.6 0.0 copy-start.5
  6.6 0.7 copy-done.5
  7.3 73.3 %shard_map.86 = (f32[8,16,128]{2,1,0:T(8,128)S(1)}, f32[8,16,128]{2,1,0:T(8,128)S(1)}) custom-call(f32[8,16,128]{2,1,0:T(8,128)S(1)} %copy-done.2, f32[8,16,128]{2,1,0:T(8,128)S(1)} %copy-done.3, s32[8,16,128]{2,1,0:T(8,128)S(1)} %copy-done.4, bf16[32,8,16,128]{3,2,1,0:T(8,128)(2,1)S(1)} %copy-done.1, s32[1,1]{1,0:T(1,128)S(6)} %copy.11.count_ref, ...), custom_call_target="tpu_custom_call" | custom-call | flops 10000000 | bytes 4000000 | tf_op jit(solution)/shard_map/pallas_call | solution.py:305
  80.6 0.6 copy.12
  81.2 0.6 copy.13
Async XLA Ops:
  1.3 1.6 %copy-start = (f32[512,1024]{1,0:T(8,128)S(1)}, f32[512,1024]{1,0:T(8,128)}, u32[]{:S(2)}) copy-start(f32[512,1024]{1,0:T(8,128)} %inv_hbm.1) | copy-start | bytes 6291460
  2.9 1.2 %copy-start.1 = (bf16[32,8,16,128]{3,2,1,0:T(8,128)(2,1)S(1)}, bf16[32,8,16,128]{3,2,1,0:T(8,128)(2,1)}, u32[]{:S(2)}) copy-start(bf16[32,8,16,128]{3,2,1,0:T(8,128)(2,1)} %vec_hbm.1) | copy-start | bytes 3145732
  4.1 0.8 %copy-start.2 = (f32[8,16,128]{2,1,0:T(8,128)S(1)}, f32[8,16,128]{2,1,0:T(8,128)}, u32[]{:S(2)}) copy-start(f32[8,16,128]{2,1,0:T(8,128)} %right_hbm.1) | copy-start | bytes 196612
  4.9 0.8 %copy-start.3 = (f32[8,16,128]{2,1,0:T(8,128)S(1)}, f32[8,16,128]{2,1,0:T(8,128)}, u32[]{:S(2)}) copy-start(f32[8,16,128]{2,1,0:T(8,128)} %diag_hbm.1) | copy-start | bytes 196612
  5.8 0.8 %copy-start.4 = (s32[8,16,128]{2,1,0:T(8,128)S(1)}, s32[8,16,128]{2,1,0:T(8,128)}, u32[]{:S(2)}) copy-start(s32[8,16,128]{2,1,0:T(8,128)} %mask_hbm.1) | copy-start | bytes 196612
  6.6 0.7 copy-start.5

commit v2 on v1

--- a/solution.py
+++ b/solution.py
@@ -30,15 +30,16 @@
 
 def kernel(
     nx, ny, kmax,
-    right_hbm, diag_hbm, mask_hbm, vec_hbm, count_ref, slot_ref, slots_ref, inv_hbm,
+    right_hbm, diag_hbm, mask_hbm, vec_hbm, slots_hbm, inv_hbm,
     sol_ref, res_ref,
     right, diag, solid, vec, inv, fluid, jac, pad,
-    parts, stack, onehot,
+    parts, stack, onehot, slot_ref, slots_ref,
     zsend, zbuf, psend, pbuf, csend, cbuf,
     xsend, xbuf, ysend, ybuf,
+    xface, xnear, yface, ynear, held,
     fsend, fzbuf, fpsend, fpbuf,
     load_sem, z_send_sem, z_recv_sem, p_send_sem, p_recv_sem, c_send_sem, c_recv_sem,
-    h_send_sem, h_recv_sem, f_send_sem, f_recv_sem,
+    h_send_sem, h_recv_sem, v_send_sem, v_recv_sem, f_send_sem, f_recv_sem,
 ):
     gx, gy = lax.axis_index("gx"), lax.axis_index("gy")
 
@@ -57,15 +58,14 @@
     loads = [
         pltpu.make_async_copy(src, dst, load_sem.at[i])
         for i, (src, dst) in enumerate(
-            [(right_hbm, right), (vec_hbm, vec), (mask_hbm, solid), (diag_hbm, diag), (inv_hbm, inv)]
+            [(right_hbm, right), (vec_hbm, vec), (mask_hbm, solid), (diag_hbm, diag), (inv_hbm, inv),
+             (slots_hbm, slot_ref), (slots_hbm, slots_ref)]
         )
     ]
     for load in loads:
         load.start()
 
-    count = count_ref[0, 0]
     lane = lane_ids((1, 128))
-    live = ((lane < count) | (lane >= kmax)).astype(F32)
 
     def remote(src, dst, send_sem, recv_sem, device):
         return pltpu.make_async_remote_copy(
@@ -103,9 +103,16 @@
             remote(ysend.at[n, 1], ybuf.at[n, 0], h_send_sem.at[n, 3], h_recv_sem.at[n, 3], along_y(1)),
         ]
 
+    def face_copies():
+        return [
+            remote(xface.at[0], xnear.at[1], v_send_sem.at[0], v_recv_sem.at[0], along_x(nx - 1)),
+            remote(xface.at[1], xnear.at[0], v_send_sem.at[1], v_recv_sem.at[1], along_x(1)),
+            remote(yface.at[0], ynear.at[1], v_send_sem.at[2], v_recv_sem.at[2], along_y(ny - 1)),
+            remote(yface.at[1], ynear.at[0], v_send_sem.at[3], v_recv_sem.at[3], along_y(1)),
+        ]
+
     def halo_start(n, field):
         masked = fluid[...] * field
-        pad[1:9, 8:24, :] = masked
         xsend[n, 0] = masked[0]
         xsend[n, 1] = masked[7]
         ysend[n, 0] = masked[:, 0, :]
@@ -113,23 +120,27 @@
         for copy in halo_copies(n):
             copy.start()
 
-    def halo_finish(n, field):
+    def halo_finish(n):
         for copy in halo_copies(n):
             copy.wait_recv()
-        zero = jnp.float32(0.0)
-        keep = [gx > 0, gx < nx - 1, gy > 0, gy < ny - 1]
-        scale = [jnp.where(k, jnp.float32(1.0), zero) for k in keep]
-        pad[0, 8:24, :] = xbuf[n, 0] * scale[0]
-        pad[9, 8:24, :] = xbuf[n, 1] * scale[1]
-        pad[1:9, 7:8, :] = (ybuf[n, 0] * scale[2]).reshape(8, 1, 128)
-        pad[1:9, 24:25, :] = (ybuf[n, 1] * scale[3]).reshape(8, 1, 128)
-        masked = pad[1:9, 8:24, :]
+        return [xbuf[n, 0], xbuf[n, 1], ybuf[n, 0], ybuf[n, 1]]
+
+    keep = [gx > 0, gx < nx - 1, gy > 0, gy < ny - 1]
+    scale = [jnp.where(k, jnp.float32(1.0), jnp.float32(0.0)) for k in keep]
+
+    def operate(field, halo):
+        fl = fluid[...]
+        masked = fl * field
+        pad[1:9, 8:24, :] = masked
+        pad[0, 8:24, :] = halo[0] * scale[0]
+        pad[9, 8:24, :] = halo[1] * scale[1]
+        pad[1:9, 7:8, :] = (halo[2] * scale[2]).reshape(8, 1, 128)
+        pad[1:9, 24:25, :] = (halo[3] * scale[3]).reshape(8, 1, 128)
         beside = pad[2:10, 8:24, :] + pad[0:8, 8:24, :]
         beside = beside + pad[1:9, 9:25, :] + pad[1:9, 7:23, :]
         lanes = lane_ids((8, 16, 128))
-        beside = beside + jnp.where(lanes == 127, zero, pltpu.roll(masked, 127, 2))
-        beside = beside + jnp.where(lanes == 0, zero, pltpu.roll(masked, 1, 2))
-        fl = fluid[...]
+        beside = beside + jnp.where(lanes == 127, 0.0, pltpu.roll(masked, 127, 2))
+        beside = beside + jnp.where(lanes == 0, 0.0, pltpu.roll(masked, 1, 2))
         return fl * ((6.0 + diag[...]) * field - beside) + (1.0 - fl) * field
 
     def project(n, cells_ref, extras):
@@ -174,18 +185,28 @@
                 acc = acc + inv[128 * c:128 * c + 128, 128 * i:128 * i + 128] * ordered[i:i + 1]
             csend[n, c:c + 1] = row_sums(acc)[0:1]
 
-    def prolong(n):
-        slot = slot_ref[gx * ny + gy]
+    def coefficients(n, sub_x, sub_y):
+        slot = slot_ref[sub_x * ny + sub_y]
         row = cbuf[n, slot // 16, pl.ds((slot // 4) % 4, 1), :]
         row = jnp.where(lane // 32 == slot % 4, row, 0.0)
         row = row + pltpu.roll(row, 32, 1)
-        row = row + pltpu.roll(row, 64, 1)
-        row = row * live
+        return row + pltpu.roll(row, 64, 1)
+
+    def prolong(n):
+        own = coefficients(n, gx, gy) * live
+        near = [
+            coefficients(n, lax.rem(gx + nx - 1, nx), gy), coefficients(n, lax.rem(gx + 1, nx), gy),
+            coefficients(n, gx, lax.rem(gy + ny - 1, ny)), coefficients(n, gx, lax.rem(gy + 1, ny)),
+        ]
         total = jnp.zeros((8, 16, 128), F32)
+        halo = [jnp.zeros((16, 128), F32), jnp.zeros((16, 128), F32), jnp.zeros((8, 128), F32), jnp.zeros((8, 128), F32)]
         for k in range(kmax):
-            weight = jnp.broadcast_to(row[:, k:k + 1], (1, 128)).reshape(1, 1, 128)
-            total = total + vec[k].astype(F32) * weight
-        return total
+            total = total + vec[k].astype(F32) * scalar(own, k).reshape(1, 1, 128)
+        for k in range(kmax):
+            for i in range(2):
+                halo[i] = halo[i] + xnear[i, k] * scalar(near[i], k)
+                halo[2 + i] = halo[2 + i] + ynear[i, k] * scalar(near[2 + i], k)
+        return total, halo
 
     rho = [1.0 / SIGMA]
     for _ in range(2):
@@ -195,10 +216,11 @@
         return rho[n] * rho[n - 1] * update + (2.0 * rho[n] / DELTA) * jac[...] * rest
 
     def scalar(row, i):
-        return jnp.broadcast_to(row[:, i:i + 1], (1, 128)).reshape(1, 1, 128)
-
-    loads[0].wait()
-    loads[1].wait()
+        return jnp.broadcast_to(row[:, i:i + 1], (1, 128))
+
+    for i in (5, 6, 0, 1):
+        loads[i].wait()
+    live = ((lane < slot_ref[nx * ny]) | (lane >= kmax)).astype(F32)
     stack[...] = jnp.zeros((128, 128), F32)
     project(0, right, [])
     loads[2].wait()
@@ -208,20 +230,33 @@
     jac[...] = 1.0 / (fl * (6.0 + diag[...]) + 1.0 - fl)
     pad[...] = jnp.zeros(pad.shape, F32)
 
+    def faces(k, carry):
+        alive = jnp.where(k < slot_ref[nx * ny], jnp.float32(1.0), jnp.float32(0.0))
+        values = vec[k].astype(F32) * (fluid[...] * alive)
+        xface[0, k] = values[0]
+        xface[1, k] = values[7]
+        yface[0, k] = values[:, 0, :]
+        yface[1, k] = values[:, 15, :]
+        return carry
+
+    lax.fori_loop(0, kmax, faces, 0)
+
     pl.semaphore_wait(barrier, nx - 1 + ny - 1)
     z_start(0)
 
-    def apply_preconditioner(n, res, h, between=None):
+    def apply_preconditioner(n, res, h):
         update = jac[...] * res / THETA
         halo_start(h, update)
         if n == 0:
+            for copy in face_copies()[2:]:
+                copy.start()
             block = gy // 2
             want = lax.broadcasted_iota(jnp.int32, (32, 128), 0)
             want = 32 * block + 4 * (want % 8) + want // 8
             for a in range(4):
                 have = slots_ref[pl.ds(128 * a, 128)].reshape(1, 128)
                 onehot[32 * a:32 * a + 32, :] = (want == have).astype(F32)
-        rest = res - halo_finish(h, update)
+        rest = res - operate(update, halo_finish(h))
         smooth = update
         update = smooth_update(1, update, rest)
         smooth = smooth + update
@@ -229,37 +264,50 @@
         wait_bytes(zbuf.at[n], z_recv_sem.at[n])
         compact(n)
         p_start(n)
-        rest = rest - halo_finish(h + 1, update)
+        if n == 0:
+            for copy in face_copies()[:2]:
+                copy.start()
+        rest = rest - operate(update, halo_finish(h + 1))
         smooth = smooth + smooth_update(2, update, rest)
+        halo_start(h + 2, smooth)
         if n == 0:
             loads[4].wait()
         wait_bytes(pbuf.at[n], p_recv_sem.at[n])
         coarse(n)
         c_start(n)
         sums = jnp.sum(pbuf[n, 4], axis=0, keepdims=True)
+        near = halo_finish(h + 2)
+        if n == 0:
+            for copy in face_copies():
+                copy.wait_recv()
         wait_bytes(cbuf.at[n], c_recv_sem.at[n])
-        return smooth + prolong(n), sums
+        fine, halo = prolong(n)
+        return smooth + fine, [a + b for a, b in zip(near, halo)], sums
 
     r0 = right[...]
-    z0, _ = apply_preconditioner(0, r0, 0)
+    z0, near, _ = apply_preconditioner(0, r0, 0)
     sol_ref[...] = z0
-    halo_start(2, z0)
-    norm_part = fold(r0 * z0)
-    q0 = halo_finish(2, z0)
+    held[0:16, :] = near[0]
+    held[16:32, :] = near[1]
+    held[32:40, :] = near[2]
+    held[40:48, :] = near[3]
+    q0 = operate(z0, near)
     res_ref[...] = q0
-    project(1, res_ref, [norm_part, fold(z0 * q0)])
+    project(1, res_ref, [fold(right[...] * z0), fold(z0 * q0)])
     z_start(1)
-    w0, sums = apply_preconditioner(1, q0, 3)
+    w0, near, sums = apply_preconditioner(1, q0, 3)
     norm0, curv0 = scalar(sums, kmax), scalar(sums, kmax + 1)
     step0 = norm0 / curv0
+    before = [held[0:16, :], held[16:32, :], held[32:40, :], held[40:48, :]]
+    near = [a - step0 * b for a, b in zip(before, near)]
+    norm0, curv0, step0 = (v.reshape(1, 1, 128) for v in (norm0, curv0, step0))
     z0, q0 = sol_ref[...], res_ref[...]
     z1 = z0 - step0 * w0
     r1 = right[...] - step0 * q0
     right[...] = r1
-    halo_start(5, z1)
     parts[0] = fold(r1 * z1)
     parts[1] = fold(z1 * q0)
-    t1 = halo_finish(5, z1)
+    t1 = operate(z1, near)
     parts[2] = fold(z1 * t1)
 
     stack[0:8, :] = jnp.sum(parts[0:8], axis=1)
@@ -274,7 +322,7 @@
     pltpu.make_async_copy(fpsend, fpbuf.at[gy], f_recv_sem.at[1]).start()
     wait_bytes(fpbuf, f_recv_sem.at[1])
     last = jnp.sum(fpbuf[...], axis=0)
-    norm1, cross, inner = scalar(last, 0), scalar(last, 1), scalar(last, 2)
+    norm1, cross, inner = (scalar(last, i).reshape(1, 1, 128) for i in range(3))
     beta = norm1 / norm0
     step1 = norm1 / (inner + 2.0 * beta * cross + beta * beta * curv0)
     sol_ref[...] = (step0 + step1 * beta) * z0 + step1 * z1
@@ -287,6 +335,8 @@
     for n in range(6):
         for copy in halo_copies(n):
             copy.wait_send()
+    for copy in face_copies():
+        copy.wait_send()
     wait_bytes(fzbuf.at[pl.ds(0, nx - 1)], f_send_sem.at[0])
     wait_bytes(fpbuf.at[pl.ds(0, ny - 1)], f_send_sem.at[1])
 
@@ -298,35 +348,38 @@
         cells = right_side.shape
         kmax = vectors.shape[0]
         hbm = pl.BlockSpec(memory_space=pl.ANY)
-        smem = pl.BlockSpec(memory_space=pltpu.SMEM)
         vmem = pl.BlockSpec(memory_space=pltpu.VMEM)
         dma = pltpu.SemaphoreType.DMA
         out = jax.ShapeDtypeStruct(cells, F32)
+        slots = jnp.concatenate([slots, jnp.broadcast_to(counts.reshape(1), (128,))])
         return pl.pallas_call(
             functools.partial(kernel, nx, ny, kmax),
             out_shape=(out, out),
-            in_specs=[hbm, hbm, hbm, hbm, smem, smem, vmem, hbm],
+            in_specs=[hbm] * 6,
             out_specs=(vmem, vmem),
             scratch_shapes=[
                 pltpu.VMEM(cells, F32), pltpu.VMEM(cells, F32), pltpu.VMEM(cells, jnp.int32),
                 pltpu.VMEM(vectors.shape, vectors.dtype), pltpu.VMEM(inverse.shape, F32),
                 pltpu.VMEM(cells, F32), pltpu.VMEM(cells, F32), pltpu.VMEM((10, 32, 128), F32),
                 pltpu.VMEM((kmax + 8, 8, 128), F32), pltpu.VMEM((128, 128), F32), pltpu.VMEM((128, 128), F32),
+                pltpu.SMEM(slots.shape, jnp.int32), pltpu.VMEM(slots.shape, jnp.int32),
                 pltpu.VMEM((2, 1, 128), F32), pltpu.VMEM((2, nx, 1, 128), F32),
                 pltpu.VMEM((2, 5, 1, 128), F32), pltpu.VMEM((2, 5, ny, 128), F32),
                 pltpu.VMEM((2, 4, 128), F32), pltpu.VMEM((2, ny, 4, 128), F32),
                 pltpu.VMEM((6, 2, 16, 128), F32), pltpu.VMEM((6, 2, 16, 128), F32),
                 pltpu.VMEM((6, 2, 8, 128), F32), pltpu.VMEM((6, 2, 8, 128), F32),
+                pltpu.VMEM((2, kmax, 16, 128), F32), pltpu.VMEM((2, kmax, 16, 128), F32),
+                pltpu.VMEM((2, kmax, 8, 128), F32), pltpu.VMEM((2, kmax, 8, 128), F32), pltpu.VMEM((48, 128), F32),
                 pltpu.VMEM((1, 128), F32), pltpu.VMEM((nx, 1, 128), F32),
                 pltpu.VMEM((1, 128), F32), pltpu.VMEM((ny, 1, 128), F32),
-                dma((5,)), dma((2,)), dma((2,)), dma((2,)), dma((2,)), dma((2,)), dma((2,)),
-                dma((6, 4)), dma((6, 4)), dma((2,)), dma((2,)),
+                dma((7,)), dma((2,)), dma((2,)), dma((2,)), dma((2,)), dma((2,)), dma((2,)),
+                dma((6, 4)), dma((6, 4)), dma((4,)), dma((4,)), dma((2,)), dma((2,)),
             ],
             compiler_params=pltpu.CompilerParams(
-                collective_id=0, has_side_effects=True, vmem_limit_bytes=32 * 1024 * 1024
+                collective_id=0, has_side_effects=True, vmem_limit_bytes=5375 * 1024 * 1024 // 100
             ),
             cost_estimate=pl.CostEstimate(flops=10_000_000, bytes_accessed=4_000_000, transcendentals=0),
-        )(right_side, diagonal, solid_mask, vectors, counts, slots, slots, inverse)
+        )(right_side, diagonal, solid_mask, vectors, slots, inverse)
 
     in_specs = (
         P("gx", "gy", None),

time: 82.2 us -> 69.7 us (0.85)
  Pallas kernels: 73.3 us -> 66.3 us
  local copies, waits for them, and re-layouts: 7.27 us -> 1.95 us
    pallas_call x1, Pallas kernels: 73.3 us -> 66.3 us  [on_device(): pl.pallas_call(functools.partial(kernel, nx, ny, kmax), out_shape=(out, o...]
    unnamed x14 -> x2, local copies, waits for them, and re-layouts: 7.27 us -> 1.26 us
where the time goes in v2:
time: 69.7 us; the launch traced here: 69.6 us
  Pallas kernels  66.3 us (95%)
  local copies, waits for them, and re-layouts  1.95 us (3%)
  between operations  1.28 us (2%)
    pallas_call x1, Pallas kernels, on_device(): pl.pallas_call(functools.partial(kernel, nx, ny, kmax), out_shape=(out, o...  66.3 us

profile of v2, /device:TPU:1, one launch (start us, length us, event | category | flops | bytes accessed | tf_op | source)
XLA Modules:
  0.0 69.6 jit_solution(7808027889981699051)
XLA Ops:
  1.3 0.7 concatenate.3.slots_hbm
  2.0 66.3 %shard_map.86 = (f32[8,16,128]{2,1,0:T(8,128)S(1)}, f32[8,16,128]{2,1,0:T(8,128)S(1)}) custom-call(f32[8,16,128]{2,1,0:T(8,128)} %right_hbm.1, f32[8,16,128]{2,1,0:T(8,128)} %diag_hbm.1, s32[8,16,128]{2,1,0:T(8,128)} %mask_hbm.1, bf16[32,8,16,128]{3,2,1,0:T(8,128)(2,1)} %vec_hbm.1, s32[640]{0:T(1024)S(1)} %concatenate.3.slots_hbm, f32[512,1024]{1,0:T(8,128)} %inv_hbm.1), custom_call_target="tpu_custom_call" | custom-call | flops 10000000 | bytes 4000000 | tf_op jit(solution)/shard_map/pallas_call | solution.py:355
  68.3 0.6 copy.12
  68.9 0.6 copy.13

commit v3 on v2

--- a/solution.py
+++ b/solution.py
@@ -12,20 +12,33 @@
 THETA = (CHEB_HI + CHEB_LO) / 2.0
 DELTA = (CHEB_HI - CHEB_LO) / 2.0
 SIGMA = THETA / DELTA
-HIGH = lax.Precision.HIGHEST
 MESH = pl.DeviceIdType.MESH
 F32 = jnp.float32
+BF16 = jnp.bfloat16
 
 
 def lane_ids(shape):
     return lax.broadcasted_iota(jnp.int32, shape, len(shape) - 1)
 
 
+def pieces(values):
+    high = values.astype(BF16)
+    rest = values - high.astype(F32)
+    middle = rest.astype(BF16)
+    return high, middle, (rest - middle.astype(F32)).astype(BF16)
+
+
 def row_sums(rows):
-    return lax.dot_general(
-        jnp.ones((8, 128), F32), rows, (((1,), (1,)), ((), ())),
-        precision=HIGH, preferred_element_type=F32,
+    ones = jnp.ones((16, 128), BF16)
+    return sum(
+        lax.dot_general(ones, piece, (((1,), (1,)), ((), ())), preferred_element_type=F32)
+        for piece in pieces(rows)
     )
+
+
+def spread_sums(rows):
+    ones = jnp.ones((128, 128), BF16)
+    return sum(jnp.dot(piece, ones, preferred_element_type=F32) for piece in pieces(rows))
 
 
 def kernel(
@@ -33,7 +46,7 @@
     right_hbm, diag_hbm, mask_hbm, vec_hbm, slots_hbm, inv_hbm,
     sol_ref, res_ref,
     right, diag, solid, vec, inv, fluid, jac, pad,
-    parts, stack, onehot, slot_ref, slots_ref,
+    parts, stack, onehot, coef, slot_ref, slots_ref,
     zsend, zbuf, psend, pbuf, csend, cbuf,
     xsend, xbuf, ysend, ybuf,
     xface, xnear, yface, ynear, held,
@@ -168,7 +181,7 @@
 
     def coarse(n):
         gathered = pbuf[n, 0:4].reshape(4 * ny, 128)
-        picked = jnp.dot(onehot[...], gathered, precision=HIGH, preferred_element_type=F32)
+        picked = sum(jnp.dot(onehot[...], piece, preferred_element_type=F32) for piece in pieces(gathered))
         group = lane_ids((32, 128)) // 32
         own = jnp.zeros((32, 128), F32)
         for a in range(4):
@@ -185,27 +198,32 @@
                 acc = acc + inv[128 * c:128 * c + 128, 128 * i:128 * i + 128] * ordered[i:i + 1]
             csend[n, c:c + 1] = row_sums(acc)[0:1]
 
-    def coefficients(n, sub_x, sub_y):
+    def coefficients(n, sub_x, sub_y, limit):
         slot = slot_ref[sub_x * ny + sub_y]
         row = cbuf[n, slot // 16, pl.ds((slot // 4) % 4, 1), :]
-        row = jnp.where(lane // 32 == slot % 4, row, 0.0)
-        row = row + pltpu.roll(row, 32, 1)
-        return row + pltpu.roll(row, 64, 1)
+        k = lax.broadcasted_iota(jnp.int32, (kmax, 128), 0)
+        mine = (lane_ids((kmax, 128)) == kmax * (slot % 4) + k) & (k < limit)
+        return jnp.where(mine, row, 0.0)
 
     def prolong(n):
-        own = coefficients(n, gx, gy) * live
-        near = [
-            coefficients(n, lax.rem(gx + nx - 1, nx), gy), coefficients(n, lax.rem(gx + 1, nx), gy),
-            coefficients(n, gx, lax.rem(gy + ny - 1, ny)), coefficients(n, gx, lax.rem(gy + 1, ny)),
+        subs = [
+            (gx, gy, slot_ref[nx * ny]),
+            (lax.rem(gx + nx - 1, nx), gy, kmax), (lax.rem(gx + 1, nx), gy, kmax),
+            (gx, lax.rem(gy + ny - 1, ny), kmax), (gx, lax.rem(gy + 1, ny), kmax),
         ]
+        coef[...] = spread_sums(jnp.concatenate([coefficients(n, *sub) for sub in subs], axis=0))
+
+        def weight(i, k):
+            return coef[i * kmax + k:i * kmax + k + 1, :]
+
         total = jnp.zeros((8, 16, 128), F32)
         halo = [jnp.zeros((16, 128), F32), jnp.zeros((16, 128), F32), jnp.zeros((8, 128), F32), jnp.zeros((8, 128), F32)]
         for k in range(kmax):
-            total = total + vec[k].astype(F32) * scalar(own, k).reshape(1, 1, 128)
+            total = total + vec[k].astype(F32) * weight(0, k).reshape(1, 1, 128)
         for k in range(kmax):
             for i in range(2):
-                halo[i] = halo[i] + xnear[i, k] * scalar(near[i], k)
-                halo[2 + i] = halo[2 + i] + ynear[i, k] * scalar(near[2 + i], k)
+                halo[i] = halo[i] + xnear[i, k] * weight(1 + i, k)
+                halo[2 + i] = halo[2 + i] + ynear[i, k] * weight(3 + i, k)
         return total, halo
 
     rho = [1.0 / SIGMA]
@@ -255,7 +273,7 @@
             want = 32 * block + 4 * (want % 8) + want // 8
             for a in range(4):
                 have = slots_ref[pl.ds(128 * a, 128)].reshape(1, 128)
-                onehot[32 * a:32 * a + 32, :] = (want == have).astype(F32)
+                onehot[32 * a:32 * a + 32, :] = (want == have).astype(F32).astype(BF16)
         rest = res - operate(update, halo_finish(h))
         smooth = update
         update = smooth_update(1, update, rest)
@@ -361,7 +379,7 @@
                 pltpu.VMEM(cells, F32), pltpu.VMEM(cells, F32), pltpu.VMEM(cells, jnp.int32),
                 pltpu.VMEM(vectors.shape, vectors.dtype), pltpu.VMEM(inverse.shape, F32),
                 pltpu.VMEM(cells, F32), pltpu.VMEM(cells, F32), pltpu.VMEM((10, 32, 128), F32),
-                pltpu.VMEM((kmax + 8, 8, 128), F32), pltpu.VMEM((128, 128), F32), pltpu.VMEM((128, 128), F32),
+                pltpu.VMEM((kmax + 8, 8, 128), F32), pltpu.VMEM((128, 128), F32), pltpu.VMEM((128, 128), BF16), pltpu.VMEM((5 * kmax, 128), F32),
                 pltpu.SMEM(slots.shape, jnp.int32), pltpu.VMEM(slots.shape, jnp.int32),
                 pltpu.VMEM((2, 1, 128), F32), pltpu.VMEM((2, nx, 1, 128), F32),
                 pltpu.VMEM((2, 5, 1, 128), F32), pltpu.VMEM((2, 5, ny, 128), F32),

time: 69.7 us -> 68.7 us (0.986)
  Pallas kernels: 66.3 us -> 65.3 us
    pallas_call x1, Pallas kernels: 66.3 us -> 65.3 us  [on_device(): pl.pallas_call(functools.partial(kernel, nx, ny, kmax), out_shape=(out, o...]
where the time goes in v3:
time: 68.7 us; the launch traced here: 68.5 us
  Pallas kernels  65.3 us (95%)
  local copies, waits for them, and re-layouts  1.95 us (3%)
  between operations  1.28 us (2%)
    pallas_call x1, Pallas kernels, on_device(): pl.pallas_call(functools.partial(kernel, nx, ny, kmax), out_shape=(out, o...  65.3 us

profile of v3, /device:TPU:1, one launch (start us, length us, event | category | flops | bytes accessed | tf_op | source)
XLA Modules:
  0.0 68.5 jit_solution(16509258652770898383)
XLA Ops:
  1.3 0.7 %concatenate.3.slots_hbm = s32[640]{0:T(1024)S(1)} pad(s32[512]{0:T(512)} %param.12, s32[]{:T(128)} %bitcast.1), padding=0_128 | pad | bytes 4612 | tf_op jit(solution)/shard_map/concatenate | solution.py:372
  2.0 65.3 %shard_map.86 = (f32[8,16,128]{2,1,0:T(8,128)S(1)}, f32[8,16,128]{2,1,0:T(8,128)S(1)}) custom-call(f32[8,16,128]{2,1,0:T(8,128)} %right_hbm.1, f32[8,16,128]{2,1,0:T(8,128)} %diag_hbm.1, s32[8,16,128]{2,1,0:T(8,128)} %mask_hbm.1, bf16[32,8,16,128]{3,2,1,0:T(8,128)(2,1)} %vec_hbm.1, s32[640]{0:T(1024)S(1)} %concatenate.3.slots_hbm, f32[512,1024]{1,0:T(8,128)} %inv_hbm.1), custom_call_target="tpu_custom_call" | custom-call | flops 10000000 | bytes 4000000 | tf_op jit(solution)/shard_map/pallas_call | solution.py:373
  67.2 0.6 copy.12
  67.9 0.6 copy.13

commit v4 on v3

--- a/solution.py
+++ b/solution.py
@@ -157,14 +157,9 @@
         return fl * ((6.0 + diag[...]) * field - beside) + (1.0 - fl) * field
 
     def project(n, cells_ref, extras):
-        def group(g, carry):
-            cells = cells_ref[...]
-            for j in range(4):
-                k = g * 4 + j
-                parts[k] = fold(vec[k].astype(F32) * cells)
-            return carry
-
-        lax.fori_loop(0, kmax // 4, group, 0)
+        cells = cells_ref[...]
+        for k in range(kmax):
+            parts[k] = fold(vec[k].astype(F32) * cells)
         for i in range(8):
             parts[kmax + i] = extras[i] if i < len(extras) else jnp.zeros((8, 128), F32)
         stack[0:kmax + 8, :] = jnp.sum(parts[...], axis=1)

time: 68.7 us -> 68.6 us (level)
  no operation moved by 1% of the time
where the time goes in v4:
time: 68.6 us; the launch traced here: 68.4 us
  Pallas kernels  65.2 us (95%)
  local copies, waits for them, and re-layouts  1.95 us (3%)
  between operations  1.28 us (2%)
    pallas_call x1, Pallas kernels, on_device(): pl.pallas_call(functools.partial(kernel, nx, ny, kmax), out_shape=(out, o...  65.2 us

profile of v4, /device:TPU:1, one launch (start us, length us, event | category | flops | bytes accessed | tf_op | source)
XLA Modules:
  0.0 68.4 jit_solution(15857679078351753791)
XLA Ops:
  1.3 0.7 %concatenate.3.slots_hbm = s32[640]{0:T(1024)S(1)} pad(s32[512]{0:T(512)} %param.12, s32[]{:T(128)} %bitcast.1), padding=0_128 | pad | bytes 4612 | tf_op jit(solution)/shard_map/concatenate | solution.py:367
  2.0 65.2 %shard_map.86 = (f32[8,16,128]{2,1,0:T(8,128)S(1)}, f32[8,16,128]{2,1,0:T(8,128)S(1)}) custom-call(f32[8,16,128]{2,1,0:T(8,128)} %right_hbm.1, f32[8,16,128]{2,1,0:T(8,128)} %diag_hbm.1, s32[8,16,128]{2,1,0:T(8,128)} %mask_hbm.1, bf16[32,8,16,128]{3,2,1,0:T(8,128)(2,1)} %vec_hbm.1, s32[640]{0:T(1024)S(1)} %concatenate.3.slots_hbm, f32[512,1024]{1,0:T(8,128)} %inv_hbm.1), custom_call_target="tpu_custom_call" | custom-call | flops 10000000 | bytes 4000000 | tf_op jit(solution)/shard_map/pallas_call | solution.py:368
  67.2 0.6 copy.12
  67.8 0.6 copy.13

commit v5 on v4

--- a/solution.py
+++ b/solution.py
@@ -28,17 +28,14 @@
     return high, middle, (rest - middle.astype(F32)).astype(BF16)
 
 
-def row_sums(rows):
-    ones = jnp.ones((16, 128), BF16)
-    return sum(
-        lax.dot_general(ones, piece, (((1,), (1,)), ((), ())), preferred_element_type=F32)
-        for piece in pieces(rows)
-    )
-
-
 def spread_sums(rows):
     ones = jnp.ones((128, 128), BF16)
     return sum(jnp.dot(piece, ones, preferred_element_type=F32) for piece in pieces(rows))
+
+
+def row_sums(rows):
+    diagonal = lane_ids((128, 128)) == lax.broadcasted_iota(jnp.int32, (128, 128), 0)
+    return jnp.sum(jnp.where(diagonal, spread_sums(rows), 0.0), axis=0, keepdims=True)
 
 
 def kernel(
@@ -163,7 +160,7 @@
         for i in range(8):
             parts[kmax + i] = extras[i] if i < len(extras) else jnp.zeros((8, 128), F32)
         stack[0:kmax + 8, :] = jnp.sum(parts[...], axis=1)
-        zsend[n] = row_sums(stack[...])[0:1] * live
+        zsend[n] = row_sums(stack[...]) * live
 
     def compact(n):
         rows = zbuf[n].reshape(nx, 128)
@@ -191,7 +188,7 @@
             acc = inv[128 * c:128 * c + 128, 0:128] * ordered[0:1]
             for i in range(1, 8):
                 acc = acc + inv[128 * c:128 * c + 128, 128 * i:128 * i + 128] * ordered[i:i + 1]
-            csend[n, c:c + 1] = row_sums(acc)[0:1]
+            csend[n, c:c + 1] = row_sums(acc)
 
     def coefficients(n, sub_x, sub_y, limit):
         slot = slot_ref[sub_x * ny + sub_y]
@@ -324,7 +321,7 @@
     parts[2] = fold(z1 * t1)
 
     stack[0:8, :] = jnp.sum(parts[0:8], axis=1)
-    fsend[...] = row_sums(stack[...])[0:1]
+    fsend[...] = row_sums(stack[...])
     for step in range(1, nx):
         remote(fsend, fzbuf.at[gx], f_send_sem.at[0], f_recv_sem.at[0], along_x(step)).start()
     pltpu.make_async_copy(fsend, fzbuf.at[gx], f_recv_sem.at[0]).start()

time: 68.6 us -> 68.6 us (level)
  no operation moved by 1% of the time
where the time goes in v5:
time: 68.6 us; the launch traced here: 68.4 us
  Pallas kernels  65.2 us (95%)
  local copies, waits for them, and re-layouts  1.95 us (3%)
  between operations  1.28 us (2%)
    pallas_call x1, Pallas kernels, on_device(): pl.pallas_call(functools.partial(kernel, nx, ny, kmax), out_shape=(out, o...  65.2 us

profile of v5, /device:TPU:1, one launch (start us, length us, event | category | flops | bytes accessed | tf_op | source)
XLA Modules:
  0.0 68.4 jit_solution(6207954592528978751)
XLA Ops:
  1.3 0.7 %concatenate.3.slots_hbm = s32[640]{0:T(1024)S(1)} pad(s32[512]{0:T(512)} %param.12, s32[]{:T(128)} %bitcast.1), padding=0_128 | pad | bytes 4612 | tf_op jit(solution)/shard_map/concatenate | solution.py:364
  2.0 65.2 %shard_map.86 = (f32[8,16,128]{2,1,0:T(8,128)S(1)}, f32[8,16,128]{2,1,0:T(8,128)S(1)}) custom-call(f32[8,16,128]{2,1,0:T(8,128)} %right_hbm.1, f32[8,16,128]{2,1,0:T(8,128)} %diag_hbm.1, s32[8,16,128]{2,1,0:T(8,128)} %mask_hbm.1, bf16[32,8,16,128]{3,2,1,0:T(8,128)(2,1)} %vec_hbm.1, s32[640]{0:T(1024)S(1)} %concatenate.3.slots_hbm, f32[512,1024]{1,0:T(8,128)} %inv_hbm.1), custom_call_target="tpu_custom_call" | custom-call | flops 10000000 | bytes 4000000 | tf_op jit(solution)/shard_map/pallas_call | solution.py:365
  67.1 0.6 copy.12
  67.8 0.6 copy.13
